TPU v7x, 256 devices: a whole 4x4x8 slice. The times are simulated.
256 devices in a mesh: ia: 16 (over x, z_hi, core), ja: 4 (over z_lo), ka: 4 (over y).
Axes of the slice: x: 4, y: 4, z: 8 (z_hi: 2, z_lo: 4; z = z_hi * 4 + z_lo), core: 2. Of those that a mesh axis runs over, the one named last changes fastest.
Arguments:
- blocks: bfloat16 [16, 4, 4, 3, 128, 128, 128], P('ia', 'ja', 'ka'), may hold values from -6 to 6
- coords: int32 [16, 4, 4, 3, 3], P('ia', 'ja', 'ka'), may hold values from 0 to 3
- counts: int32 [16, 4, 4], P('ia', 'ja', 'ka'), may hold values from 1 to 3, as said below
- b_factor: float32 [4, 512, 256], P('ja', ('ia', 'ka')), may hold values from -50 to 100
- c_factor: float32 [4, 512, 256], P('ka', ('ia', 'ja')), may hold values from -50 to 100
Outputs:
- a_new: float32 [16, 512, 256], P('ia', ('ja', 'ka'))
- b_new: float32 [4, 512, 256], P('ja', ('ia', 'ka'))
Inputs may be any that keep to these rules, and one draw needn't show every extreme that they name: Only the first counts slots of a cell hold live blocks; the other slots are ignored. Some cell is full in every draw. `coords`: row blocks are local to the cell's slab of each mode; one cell may name the same row block in several slots.
All inputs are finite; a program needn't handle non-finite values.
Results may differ from a plain program's by a relative error of at most 0.007.
Values may be sent and summed in bfloat16 or wider, within the bound.
No kernel may reach another device: no remote copies, remote signals or barrier semaphores. Data moves between devices by JAX's collectives and lax.ppermute only.
A program may use at most 128 MiB of HBM per device.

v0:
```python
import jax
import jax.numpy as jnp
from jax import lax
from jax.sharding import PartitionSpec as P


def solve_right(matrix, hadamard):
    factor_low = jnp.linalg.cholesky(hadamard)
    partial_solve = lax.linalg.triangular_solve(
        factor_low, matrix, left_side=False, lower=True, transpose_a=True
    )
    return lax.linalg.triangular_solve(
        factor_low, partial_solve, left_side=False, lower=True, transpose_a=False
    )


def gram_of(matrix):
    return jnp.dot(
        matrix.T, matrix, precision=lax.Precision.HIGHEST, preferred_element_type=jnp.float32
    )


def local(blocks, coords, counts, b_factor, c_factor):
    local_blocks = blocks[0, 0, 0]
    local_coords = coords[0, 0, 0]
    live_count = counts[0, 0, 0]
    b_owned = b_factor[0]
    c_owned = c_factor[0]
    rank_width = b_owned.shape[1]
    block_size = local_blocks.shape[1]
    all_devices = lax.axis_size(("ia", "ja", "ka"))
    rows_b = b_owned.shape[0] * all_devices
    rows_c = c_owned.shape[0] * all_devices
    raw_b, raw_c = lax.psum((gram_of(b_owned), gram_of(c_owned)), ("ia", "ja", "ka"))
    gram_b = raw_b / rows_b
    gram_c = raw_c / rows_c
    c_slab = lax.all_gather(c_owned.astype(jnp.bfloat16), ("ia", "ja"), axis=0, tiled=True)
    b_slab = lax.all_gather(b_owned.astype(jnp.bfloat16), ("ia", "ka"), axis=0, tiled=True)
    slab_rows = c_slab.shape[0]

    def product(slot_index):
        tensor_block = lax.dynamic_index_in_dim(local_blocks, slot_index, 0, keepdims=False)
        c_block = lax.dynamic_slice_in_dim(
            c_slab, local_coords[slot_index, 2] * block_size, block_size, 0
        )
        flat_prod = jnp.dot(
            tensor_block.reshape(block_size * block_size, block_size),
            c_block,
            preferred_element_type=jnp.float32,
        )
        return flat_prod.astype(jnp.bfloat16).reshape(block_size, block_size, rank_width)

    kept_products = jnp.zeros((1, 1, 1, rank_width), jnp.bfloat16)

    def mode_one(slot_index, state_pair):
        summed, stored = state_pair
        product_block = product(slot_index)
        b_block = lax.dynamic_slice_in_dim(
            b_slab, local_coords[slot_index, 1] * block_size, block_size, 0
        )
        contrib = jnp.einsum(
            "pqr,qr->pr", product_block, b_block, preferred_element_type=jnp.float32
        )
        row_start = local_coords[slot_index, 0] * block_size
        previous = lax.dynamic_slice_in_dim(summed, row_start, block_size, 0)
        summed = lax.dynamic_update_slice_in_dim(summed, previous + contrib, row_start, 0)
        return (summed, stored)

    m_a, kept_products = lax.fori_loop(
        0, live_count, mode_one, (jnp.zeros((slab_rows, rank_width), jnp.float32), kept_products)
    )
    a_terms = lax.psum_scatter(m_a, ("ja", "ka"), scatter_dimension=0, tiled=True)
    unscaled_a = solve_right(a_terms, gram_b * gram_c)
    rows_a = unscaled_a.shape[0] * all_devices
    squares_a = lax.psum(jnp.sum(unscaled_a * unscaled_a, axis=0), ("ia", "ja", "ka"))
    scale_a = jnp.sqrt(squares_a / rows_a + 1e-06)
    a_new = unscaled_a / scale_a
    gram_a = lax.psum(gram_of(a_new), ("ia", "ja", "ka")) / rows_a
    a_slab = lax.all_gather(a_new.astype(jnp.bfloat16), ("ja", "ka"), axis=0, tiled=True)

    def mode_two(slot_index, summed):
        product_block = product(slot_index)
        a_block = lax.dynamic_slice_in_dim(
            a_slab, local_coords[slot_index, 0] * block_size, block_size, 0
        )
        contrib = jnp.einsum(
            "pqr,pr->qr", product_block, a_block, preferred_element_type=jnp.float32
        )
        row_start = local_coords[slot_index, 1] * block_size
        previous = lax.dynamic_slice_in_dim(summed, row_start, block_size, 0)
        return lax.dynamic_update_slice_in_dim(summed, previous + contrib, row_start, 0)

    m_b = lax.fori_loop(0, live_count, mode_two, jnp.zeros((slab_rows, rank_width), jnp.float32))
    b_terms = lax.psum_scatter(m_b, ("ia", "ka"), scatter_dimension=0, tiled=True)
    unscaled_b = solve_right(b_terms, gram_a * gram_c)
    squares_b = lax.psum(jnp.sum(unscaled_b * unscaled_b, axis=0), ("ia", "ja", "ka"))
    b_new = unscaled_b / jnp.sqrt(squares_b / rows_b + 1e-06)
    return (a_new[None], b_new[None])


def solution(mesh):
    return jax.shard_map(
        local,
        mesh=mesh,
        in_specs=(
            P("ia", "ja", "ka", None, None, None, None),
            P("ia", "ja", "ka", None, None),
            P("ia", "ja", "ka"),
            P("ja", ("ia", "ka"), None),
            P("ka", ("ia", "ja"), None),
        ),
        out_specs=(P("ia", ("ja", "ka"), None), P("ja", ("ia", "ka"), None)),
        check_vma=False,
    )
```

profile of v0, /device:TPU:2, one launch (start us, length us, event | category | flops | bytes accessed | tf_op | source)
XLA Modules:
  0.0 1310.0 jit_solution(3090815077085541142)
XLA Ops:
  13.3 109.0 %all_gather.10 = bf16[512,256]{1,0:T(8,128)(2,1)S(1)} all-gather(bf16[8,256]{1,0:T(8,128)(2,1)S(1)} %bitcast_convert_fusion.2), channel_id=1, replica_groups=mesh['ia'=16,'ja'=4,'ka'=4] {'ia','ja'}, dimensions={0}, use_global_device_ids=true | all-gather | bytes 266240 | tf_op jit(solution)/shard_map/all_gather | solution.py:37
  123.0 191.3 %all_gather.9 = bf16[512,256]{1,0:T(8,128)(2,1)S(1)} all-gather(bf16[8,256]{1,0:T(8,128)(2,1)S(1)} %bitcast_convert_fusion.3), channel_id=1, replica_groups=mesh['ia'=16,'ja'=4,'ka'=4] {'ia','ka'}, dimensions={0}, use_global_device_ids=true | all-gather | bytes 266240 | tf_op jit(solution)/shard_map/all_gather | solution.py:38
  314.3 8.8 while.22
  316.9 2.5 constant_dynamic-slice_fusion.17
  325.8 11.7 cholesky.130
  337.6 9.8 custom-call.21
  347.9 11.7 cholesky.147
  361.6 4.0 while.24
  365.6 19.7 %custom-call.18 = f32[2,128,128]{1,2,0:T(8,128)S(1)} custom-call(f32[2,128,128]{2,1,0:T(8,128)S(1)} %get-tuple-element.88), custom_call_target="InvertDiagBlocksLowerTriangular" | custom-call | tf_op jit(solution)/shard_map/triangular_solve | solution.py:9
  385.3 65.4 %reduce-scatter.3.cloned.1.call-done = f32[32,256]{1,0:T(8,128)} async-done(((f32[512,256]{1,0:T(8,128)}), f32[32,256]{1,0:T(8,128)}) %reduce-scatter.3.cloned.1.call-update) | async-done | bytes 32784 | tf_op jit(solution)/shard_map/reduce_scatter | solution.py:72
  453.4 73.0 %psum.37 = f32[256]{0:T(256)S(1)} all-reduce(f32[256]{0:T(256)S(1)} %multiply_reduce_fusion.2), channel_id=1, replica_groups=mesh['ia'=16,'ja'=4,'ka'=4] {'ia','ja','ka'}, use_global_device_ids=true, to_apply=%region_10.12 | all-reduce | flops 256 | bytes 2048 | tf_op jit(solution)/shard_map/psum | solution.py:75
  527.5 41.5 %all_gather.11 = bf16[512,256]{1,0:T(8,128)(2,1)S(1)} all-gather(bf16[32,256]{1,0:T(8,128)(2,1)S(1)} %fusion.35), channel_id=1, replica_groups=mesh['ia'=16,'ja'=4,'ka'=4] {'ja','ka'}, dimensions={0}, use_global_device_ids=true | all-gather | bytes 278528 | tf_op jit(solution)/shard_map/all_gather | solution.py:79
  569.1 17.8 %while.23 = (s32[]{:T(128)}, f32[512,256]{1,0:T(8,128)S(1)}, s32[]{:T(128)}, s32[3,3]{1,0:T(4,128)S(1)}, bf16[512,256]{1,0:T(8,128)(2,1)S(1)}, /*index=5*/bf16[3...) while((s32[]{:T(128)}, f32[512,256]{1,0:T(8,128)S(1)}, ...), condition=%wide.region_12.14_spmd, body=%wide.region_11.13_spmd.sunk | while | flops 1090551808 | bytes 30277964 | solution.py:93
  571.2 2.5 constant_dynamic-slice_fusion.19
  573.7 5.6 convolution_convert_fusion.3
  579.9 5.5 multiply_reduce_fusion.6
  588.3 225.8 %all-reduce.5.cloned.1.call-done = f32[256,256]{0,1:T(8,128)} async-done(((f32[256,256]{0,1:T(8,128)}), f32[256,256]{0,1:T(8,128)}) %all-reduce.5.cloned.1.call-update) | async-done | bytes 262160 | tf_op jit(solution)/shard_map/psum | solution.py:78
  815.3 11.7 cholesky.164
  827.1 9.8 custom-call.22
  837.4 11.7 cholesky.181
  851.7 4.1 while.25
  855.8 19.7 %custom-call.19 = f32[2,128,128]{1,2,0:T(8,128)S(1)} custom-call(f32[2,128,128]{2,1,0:T(8,128)S(1)} %get-tuple-element.96), custom_call_target="InvertDiagBlocksLowerTriangular" | custom-call | tf_op jit(solution)/shard_map/triangular_solve | solution.py:9
  875.5 313.2 %reduce-scatter.5.cloned.1.call-done = f32[8,256]{1,0:T(8,128)} async-done(((f32[512,256]{1,0:T(8,128)}), f32[8,256]{1,0:T(8,128)}) %reduce-scatter.5.cloned.1.call-update) | async-done | bytes 8208 | tf_op jit(solution)/shard_map/reduce_scatter | solution.py:94
  1191.2 110.8 %psum.39 = f32[256]{0:T(256)S(1)} all-reduce(f32[256]{0:T(256)S(1)} %fusion.28), channel_id=1, replica_groups=mesh['ia'=16,'ja'=4,'ka'=4] {'ia','ja','ka'}, use_global_device_ids=true, to_apply=%region_16.18 | all-reduce | flops 256 | bytes 2048 | tf_op jit(solution)/shard_map/psum | solution.py:96
  (88 shorter events, 32.9 us)
Async XLA Ops:
  8.0 316.6 %all-reduce.7.cloned.1.call-start = ((), (), s32[]{:S(2)}) async-start(), calls=%async_computation.5 | async-start | bytes 1048576 | tf_op jit(solution)/shard_map/psum | solution.py:34
  11.9 438.8 %reduce-scatter.3.cloned.1.call-start = ((), (), s32[]{:S(2)}) async-start(), calls=%async_computation.2 | async-start | bytes 557056 | tf_op jit(solution)/shard_map/reduce_scatter | solution.py:72
  323.2 0.8 copy-start
  324.0 490.1 %all-reduce.5.cloned.1.call-start = ((), (), s32[]{:S(2)}) async-start(), calls=%async_computation.4 | async-start | bytes 524288 | tf_op jit(solution)/shard_map/psum | solution.py:78
  569.0 619.6 %reduce-scatter.5.cloned.1.call-start = ((), (), s32[]{:S(2)}) async-start(), calls=%async_computation.3 | async-start | bytes 532480 | tf_op jit(solution)/shard_map/reduce_scatter | solution.py:94
  569.1 245.0 %copy-start.2 = (f32[256,256]{0,1:T(8,128)S(1)}, f32[256,256]{0,1:T(8,128)}, u32[]{:S(2)}) copy-start(f32[256,256]{0,1:T(8,128)} %get-tuple-element.142) | copy-start | bytes 786436
  586.9 0.8 copy-start.1
Sparse Core Ops, SparseCore 0:
  14.5 256.7 all-reduce.6
  569.1 244.9 all-reduce.4
  816.8 371.8 reduce-scatter.4
Sparse Core Ops, SparseCore 1:
  324.1 126.6 reduce-scatter.2
where the time goes:
time: 1310 us
  waiting for transfers between devices  604 us (46%)
  blocking collectives  525 us (40%)
  other arithmetic  118 us (9%)
  matrix products  18.9 us (1%)
  between operations  18.2 us (1%)
  local copies, waits for them, and re-layouts  16.6 us (1%)
    reduce_scatter x1, waiting for transfers between devices, local(): lax.psum_scatter(m_b, ('ia', 'ka'), scatter_dimension=0, tiled=True)  313 us
    psum x1, waiting for transfers between devices, local(): gram_a = lax.psum(gram_of(a_new), ('ia', 'ja', 'ka')) / rows_a  226 us
    all_gather x1, blocking collectives, local(): lax.all_gather(b_owned.astype(jnp.bfloat16), ('ia', 'ka'), axis=0, tiled=...  191 us
    psum x1, blocking collectives, local(): lax.psum(jnp.sum(unscaled_b * unscaled_b, axis=0), ('ia', 'ja', 'ka'))  111 us
    all_gather x1, blocking collectives, local(): lax.all_gather(c_owned.astype(jnp.bfloat16), ('ia', 'ja'), axis=0, tiled=...  109 us
    psum x1, blocking collectives, local(): lax.psum(jnp.sum(unscaled_a * unscaled_a, axis=0), ('ia', 'ja', 'ka'))  73 us
    another operation x13, other arithmetic, solve_right(): factor_low = jnp.linalg.cholesky(hadamard)  68.6 us
    reduce_scatter x1, waiting for transfers between devices, local(): lax.psum_scatter(m_a, ('ja', 'ka'), scatter_dimension=0, tiled=True)  65.4 us
  transfers between devices with their start and end apart: 4, of which 3 were waited for; matrix products, arithmetic and copies ran while one was open for 11% of the time, Pallas kernels for 0%

commit v1 on v0

v1 whole, which is shorter than its diff:
```python
import functools

import jax
import jax.numpy as jnp
from jax import lax
from jax.experimental import pallas as pl
from jax.experimental.pallas import tpu as pltpu
from jax.sharding import PartitionSpec as P

NX, NH, NC, NJ, NK = 4, 2, 2, 4, 4
AXES = ("ia", "ja", "ka")
F32, BF16 = jnp.float32, jnp.bfloat16
CHUNK = 16
EDGE = 32


def flat_index(place):
    x, h, c, j, k = place
    return (((x * NH + h) * NC + c) * NJ + j) * NK + k


PLACES = [
    (x, h, c, j, k)
    for x in range(NX)
    for h in range(NH)
    for c in range(NC)
    for j in range(NJ)
    for k in range(NK)
]


def send(value, move):
    return lax.ppermute(value, AXES, [(flat_index(p), flat_index(move(p))) for p in PLACES])


def flip_core(p):
    return (p[0], p[1], 1 - p[2], p[3], p[4])


def flip_half(p):
    return (p[0], 1 - p[1], p[2], p[3], p[4])


def along_x(s, p):
    return ((p[0] + s) % NX, p[1], p[2], p[3], p[4])


def along_j(s, p):
    return (p[0], p[1], p[2], (p[3] + s) % NJ, p[4])


def along_k(s, p):
    return (p[0], p[1], p[2], p[3], (p[4] + s) % NK)


def k_or_j(s, p):
    return along_k(s, p) if p[2] == 0 else along_j(s, p)


def j_or_k(s, p):
    return along_j(s, p) if p[2] == 0 else along_k(s, p)


def ring_shifts(value, move):
    return [value] + [send(value, functools.partial(move, s)) for s in (1, 2, 3)]


def ring_gather(value, move, me, axis=0):
    got = ring_shifts(value, move)
    return jnp.stack([lax.select_n(lax.rem(me - t + 4, 4), *got) for t in range(4)], axis)


def ring_sum(value, move):
    got = ring_shifts(value, move)
    return (got[0] + got[1]) + (got[2] + got[3])


def ring_scatter(value, move, me):
    part = lambda s: lax.dynamic_index_in_dim(value, lax.rem(me + s, 4), 0, keepdims=False)
    got = [send(part(s), functools.partial(move, s)) for s in (1, 2, 3)]
    return (part(0) + got[0]) + (got[1] + got[2])


def dot_full(a, b):
    return jnp.dot(a, b, precision=lax.Precision.HIGHEST, preferred_element_type=F32)


def gram_of(rows):
    return lax.dot_general(
        rows, rows, (((0,), (0,)), ((), ())),
        precision=lax.Precision.HIGHEST, preferred_element_type=F32,
    )


def small_inverse(d):
    n = d.shape[0]
    lane = lax.broadcasted_iota(jnp.int32, d.shape, 1)
    sub = lax.broadcasted_iota(jnp.int32, d.shape, 0)
    for k in range(n):
        col = jnp.broadcast_to(d[:, k : k + 1], d.shape)
        pivot = 1.0 / col[k : k + 1, :]
        row = jnp.where(lane[:1] == k, pivot, d[k : k + 1, :] * pivot)
        d = jnp.where(sub == k, row, jnp.where(lane == k, 0.0, d) - col * row)
    return d


def inverse_body(h_ref, out_ref):
    n = h_ref.shape[0]
    out_ref[...] = h_ref[...]
    for s in range(0, n, EDGE):
        block = slice(s, s + EDGE)
        inv = small_inverse(out_ref[block, block])
        panel = out_ref[:, block]
        row = dot_full(inv, out_ref[block, :])
        out_ref[...] = out_ref[...] - dot_full(panel, row)
        out_ref[:, block] = -dot_full(panel, inv)
        out_ref[block, :] = row
        out_ref[block, block] = inv


def spd_inverse(h):
    n = h.shape[0]
    return pl.pallas_call(
        inverse_body,
        out_shape=jax.ShapeDtypeStruct((n, n), F32),
        in_specs=[pl.BlockSpec(memory_space=pltpu.VMEM)],
        out_specs=pl.BlockSpec(memory_space=pltpu.VMEM),
        cost_estimate=pl.CostEstimate(flops=2 * n**3, bytes_accessed=8 * n * n, transcendentals=0),
        name="spd_inverse",
    )(h)


def block_specs(slots, size, rank, slab):
    chunks = size // CHUNK

    def pick(n, p, count, coords):
        live = n < count[0]
        return (jnp.minimum(n, count[0] - 1), jnp.where(live, p, chunks - 1), 0, 0)

    whole = pl.BlockSpec((slab, rank), lambda n, p, count, coords: (0, 0))
    return chunks, pl.BlockSpec((1, CHUNK, size, size), pick), whole


def mode_one_body(count, coords, x_ref, b_ref, c_ref, out_ref):
    n, p = pl.program_id(0), pl.program_id(1)
    size = x_ref.shape[-1]
    rank = c_ref.shape[-1]

    @pl.when((n == 0) & (p == 0))
    def _():
        out_ref[...] = jnp.zeros_like(out_ref)

    @pl.when(n < count[0])
    def _():
        c_rows = c_ref[pl.ds(pl.multiple_of(coords[n, 2] * size, size), size), :]
        b_rows = b_ref[pl.ds(pl.multiple_of(coords[n, 1] * size, size), size), :].astype(F32)
        x = x_ref[0].reshape(CHUNK * size, size)
        prod = jnp.dot(x, c_rows, preferred_element_type=F32).astype(BF16).astype(F32)
        part = jnp.sum(prod.reshape(CHUNK, size, rank) * b_rows[None], axis=1)
        rows = pl.ds(pl.multiple_of(coords[n, 0] * size + p * CHUNK, CHUNK), CHUNK)
        out_ref[rows, :] += part


def mode_two_body(count, coords, x_ref, a_ref, c_ref, out_ref):
    n, p = pl.program_id(0), pl.program_id(1)
    size = x_ref.shape[-1]
    rank = c_ref.shape[-1]

    @pl.when((n == 0) & (p == 0))
    def _():
        out_ref[...] = jnp.zeros_like(out_ref)

    @pl.when(n < count[0])
    def _():
        c_rows = c_ref[pl.ds(pl.multiple_of(coords[n, 2] * size, size), size), :]
        a_rows = a_ref[pl.ds(pl.multiple_of(coords[n, 0] * size + p * CHUNK, CHUNK), CHUNK), :]
        x = x_ref[0].reshape(CHUNK * size, size)
        prod = jnp.dot(x, c_rows, preferred_element_type=F32).astype(BF16).astype(F32)
        part = jnp.sum(prod.reshape(CHUNK, size, rank) * a_rows.astype(F32)[:, None, :], axis=0)
        rows = pl.ds(pl.multiple_of(coords[n, 1] * size, size), size)
        out_ref[rows, :] += part


def mode_update(body, count, coords, blocks, factor, c_slab, name):
    slots, size = blocks.shape[0], blocks.shape[-1]
    slab, rank = c_slab.shape
    chunks, block_spec, whole = block_specs(slots, size, rank, slab)
    return pl.pallas_call(
        body,
        grid_spec=pltpu.PrefetchScalarGridSpec(
            num_scalar_prefetch=2,
            grid=(slots, chunks),
            in_specs=[block_spec, whole, whole],
            out_specs=whole,
        ),
        out_shape=jax.ShapeDtypeStruct((slab, rank), F32),
        compiler_params=pltpu.CompilerParams(vmem_limit_bytes=40 * 2**20),
        cost_estimate=pl.CostEstimate(
            flops=2 * slots * size**3 * rank, bytes_accessed=2 * blocks.size, transcendentals=0
        ),
        name=name,
    )(count, coords, blocks, factor, c_slab)


def local(blocks, coords, counts, b_factor, c_factor):
    blocks, coords, count = blocks[0, 0, 0], coords[0, 0, 0], counts[0, 0]
    ia, j, k = (lax.axis_index(name) for name in AXES)
    x, half, core = ia // (NH * NC), ia // NC % NH, ia % NC
    first = core == 0
    piece, rank = b_factor.shape[1:]
    slab = piece * NX * NH * NC * NK
    rows_a = slab * NX * NH * NC
    rows_b = slab * NJ
    rows_c = slab * NK

    mine = jnp.where(first, b_factor[0], c_factor[0])
    other = send(jnp.where(first, c_factor[0], b_factor[0]), flip_core)
    pair = jnp.stack([jnp.where(first, mine, other), jnp.where(first, other, mine)])
    got = send(pair, flip_half)
    quad = jnp.stack([jnp.where(half == 0, pair, got), jnp.where(half == 0, got, pair)])
    ring = ring_gather(quad, k_or_j, jnp.where(first, k, j), axis=2)
    own_slab = ring_gather(ring, along_x, x).reshape(slab, rank)
    own_half = own_slab.astype(BF16)
    other_half = send(own_half, flip_core)
    b_slab = jnp.where(first, own_half, other_half)
    c_slab = jnp.where(first, other_half, own_half)

    own_gram = ring_sum(gram_of(own_slab), j_or_k) * jnp.where(first, 1.0 / rows_b, 1.0 / rows_c)
    other_gram = send(own_gram, flip_core)
    gram_c = jnp.where(first, other_gram, own_gram)
    inverse_one = spd_inverse(own_gram * other_gram)

    m_a = mode_update(mode_one_body, count, coords, blocks, b_slab, c_slab, "mode_one")
    quarter = slab // NK
    m_a = ring_scatter(m_a.reshape(NK, quarter, rank), along_k, k)
    m_a = ring_sum(m_a, along_j)
    m_a = ring_gather(m_a, along_k, k).reshape(slab, rank)
    unscaled_a = dot_full(m_a, inverse_one)

    part = gram_of(unscaled_a).reshape(2, rank // 2, rank)
    keep = lax.dynamic_index_in_dim(part, core, 0, keepdims=False)
    give = lax.dynamic_index_in_dim(part, 1 - core, 0, keepdims=False)
    part = keep + send(give, flip_core)
    part = ring_sum(part, along_x)
    part = part + send(part, flip_half)
    other = send(part, flip_core)
    raw_a = jnp.concatenate([jnp.where(first, part, other), jnp.where(first, other, part)])
    raw_a = raw_a / rows_a
    squares_a = jnp.sum(jnp.where(jnp.eye(rank, dtype=bool), raw_a, 0.0), axis=0)
    scale_a = jnp.sqrt(squares_a + 1e-06)
    own_rows = slab // (NJ * NK)
    a_new = lax.dynamic_slice_in_dim(unscaled_a, (j * NK + k) * own_rows, own_rows, 0) / scale_a
    gram_a = raw_a / (scale_a[:, None] * scale_a[None, :])
    inverse_two = spd_inverse(gram_a * gram_c)

    m_b = mode_update(mode_two_body, count, coords, blocks, unscaled_a.astype(BF16), c_slab, "mode_two")
    m_b = jnp.moveaxis(m_b.reshape(NX * NH, NC, NK, piece, rank), (1, 2), (0, 1))
    keep = lax.dynamic_index_in_dim(m_b, core, 0, keepdims=False)
    give = lax.dynamic_index_in_dim(m_b, 1 - core, 0, keepdims=False)
    m_b = keep + send(give, flip_core)
    m_b = ring_scatter(m_b, along_k, k)
    m_b = m_b + send(m_b, flip_half)
    m_b = ring_sum(m_b, along_x)
    m_b = m_b.reshape(NX * NH * piece, rank) / scale_a
    unscaled_b = dot_full(m_b, inverse_two)
    squares_b = jnp.sum(unscaled_b * unscaled_b, axis=0, keepdims=True)
    squares_b = squares_b + send(squares_b, flip_core)
    squares_b = ring_sum(squares_b, along_k)
    squares_b = ring_sum(squares_b, along_j)
    b_new = lax.dynamic_slice_in_dim(unscaled_b, (x * NH + half) * piece, piece, 0)
    b_new = b_new / jnp.sqrt(squares_b / rows_b + 1e-06)
    return (a_new[None], b_new[None])


def solution(mesh):
    return jax.shard_map(
        local,
        mesh=mesh,
        in_specs=(
            P("ia", "ja", "ka", None, None, None, None),
            P("ia", "ja", "ka", None, None),
            P("ia", "ja", "ka"),
            P("ja", ("ia", "ka"), None),
            P("ka", ("ia", "ja"), None),
        ),
        out_specs=(P("ia", ("ja", "ka"), None), P("ja", ("ia", "ka"), None)),
        check_vma=False,
    )
```

time: 1310 us -> 232 us (0.18)
  waiting for transfers between devices: 604 us -> 40 us
  blocking collectives: 525 us -> 0 us
  other arithmetic: 118 us -> 4.89 us
  starting transfers between devices: 0.69 us -> 99.4 us
  Pallas kernels: 0 us -> 67.9 us
  between operations: 18.2 us -> 1.84 us
  matrix products: 18.9 us -> 4.81 us
    reduce_scatter x2 -> x0, waiting for transfers between devices: 379 us -> none  [the longest x1 313 us: local(): lax.psum_scatter(m_b, ('ia', 'ka'), scatter_dimension=0, tiled=True)]
    all_gather x3 -> x0, blocking collectives: 342 us -> none  [the longest x1 191 us: local(): lax.all_gather(b_owned.astype(jnp.bfloat16), ('ia', 'ka'), axis=0, tiled=...]
    psum x2 -> x0, waiting for transfers between devices: 226 us -> none  [the longest x1 226 us: local(): gram_a = lax.psum(gram_of(a_new), ('ia', 'ja', 'ka')) / rows_a]
    psum x2 -> x0, blocking collectives: 184 us -> none  [the longest x1 111 us: local(): lax.psum(jnp.sum(unscaled_b * unscaled_b, axis=0), ('ia', 'ja', 'ka'))]
    another operation x18 -> x11, other arithmetic: 108 us -> 0.94 us  [the longest x2 0.71 us: local(): jnp.stack([jnp.where(first, mine, other), jnp.where(first, other, mine)])]
    ppermute x0 -> x43, starting transfers between devices: none -> 99.4 us  [send(): lax.ppermute(value, AXES, [(flat_index(p), flat_index(move(p))) for p in...]
    pallas_call x0 -> x4, Pallas kernels: none -> 67.9 us  [the longest x2 58.2 us: spd_inverse(): pl.pallas_call(inverse_body, out_shape=jax.ShapeDtypeStruct((n, n), F32),...]
    ppermute x0 -> x43, waiting for transfers between devices: none -> 40 us  [send(): lax.ppermute(value, AXES, [(flat_index(p), flat_index(move(p))) for p in...]
  transfers between devices with their start and end apart: 4 -> 43, of which waited for: 3 -> 18; matrix products, arithmetic and copies ran while one was open for 11% -> 2% of each run, Pallas kernels for 0% -> 28%
where the time goes in v1:
time: 232 us; the launch traced here: 229 us
  starting transfers between devices  99.4 us (43%)
  Pallas kernels  67.9 us (29%)
  waiting for transfers between devices  40 us (17%)
  local copies, waits for them, and re-layouts  9.92 us (4%)
  other arithmetic  4.89 us (2%)
  matrix products  4.81 us (2%)
    ppermute x43, starting transfers between devices, send(): lax.ppermute(value, AXES, [(flat_index(p), flat_index(move(p))) for p in...  99.4 us
    pallas_call x2, Pallas kernels, spd_inverse(): pl.pallas_call(inverse_body, out_shape=jax.ShapeDtypeStruct((n, n), F32),...  58.2 us
    ppermute x43, waiting for transfers between devices, send(): lax.ppermute(value, AXES, [(flat_index(p), flat_index(move(p))) for p in...  40 us
    unnamed x5, local copies, waits for them, and re-layouts  9.83 us
    pallas_call x2, Pallas kernels, mode_update(): pl.pallas_call(body, grid_spec=pltpu.PrefetchScalarGridSpec(num_scalar_pr...  9.62 us
  transfers between devices with their start and end apart: 43, of which 18 were waited for; matrix products, arithmetic and copies ran while one was open for 2% of the time, Pallas kernels for 28%

profile of v1, /device:TPU:2, one launch (start us, length us, event | category | flops | bytes accessed | tf_op | source)
XLA Modules:
  0.0 228.7 jit_solution(1278062962056995120)
XLA Ops:
  3.2 7.2 %collective-permute-start.1 = (f32[2,8,256]{2,1,0:T(8,128)S(1)}, f32[2,8,256]{2,1,0:T(8,128)S(1)}, u32[]{:S(2)}, u32[]{:S(2)}) collective-permute-start(f32[2,8,256]{2,1,0:T(8,128)S(1)} %pad_maximum_fusion.5), channel_id=1, source_target_pairs={{0,32},{1,33},{2,34},{3,35},{4,36},{5,37},{6,38},{7,39},{8,40},{9,... | collective-permute-start | bytes 49160 | tf_op jit(solution)/shard_map/ppermute | solution.py:33
  13.8 2.9 %collective-permute-start.3 = (f32[2,2,8,256]{3,2,1,0:T(8,128)S(1)}, f32[2,2,8,256]{3,2,1,0:T(8,128)S(1)}, u32[]{:S(2)}, u32[]{:S(2)}) collective-permute-start(f32[2,2,8,256]{3,2,1,0:T(8,128)S(1)} %pad_maximum_fusion.4), channel_id=1, source_target_pairs={{0,2},{1,3},{2,0},{3,1},{4,6},{5,7},{6,4},{7,5},{8,10},{9,11},{10,... | collective-permute-start | bytes 98312 | tf_op jit(solution)/shard_map/ppermute | solution.py:33
  25.7 3.1 %collective-permute-done.6 = f32[2,2,4,8,256]{4,3,2,1,0:T(8,128)S(1)} collective-permute-done((f32[2,2,4,8,256]{4,3,2,1,0:T(8,128)S(1)}, f32[2,2,4,8,256]{4,3,2,1,0:T(8,128)S(1)}, u32[]{:S(2)}, u32[]{:S(2)}) %collective-permute-start.6) | collective-permute-done | bytes 131104 | tf_op jit(solution)/shard_map/ppermute | solution.py:33
  31.6 4.6 %copy-done = bf16[1,1,1,3,128,128,128]{6,5,4,3,2,1,0:T(8,128)(2,1)S(1)} copy-done((bf16[1,1,1,3,128,128,128]{6,5,4,3,2,1,0:T(8,128)(2,1)S(1)}, bf16[1,1,1,3,128,128,128]{6,5,4,3,2,1,0:T(8,128)(2,1)}, u32[]{:S(2)}) %copy-start) | copy-done | bytes 12582936
  36.1 4.7 %mode_one.1 = f32[512,256]{1,0:T(8,128)S(1)} custom-call(s32[1]{0:T(128)} %bitcast.113.count, s32[3,3]{1,0:T(4,128)S(1)} %bitcast.121, bf16[3,128,128,128]{3,2,1,0:T(8,128)(2,1)S(1)} %bitcast.115, bf16[512,256]{1,0:T(8,128)(2,1)S(1)} %get-tuple-element.10.b_ref, bf16[512,256]{1,0:T(8,128)(2,1)S(1)} %get-tuple-element.9.c_ref), custom_call_target="tpu_custom_call" | custom-call | flops 3221225472 | bytes 12582912 | tf_op jit(solution)/shard_map/mode_one/pallas_call | solution.py:188
  42.5 8.5 %collective-permute-start.11 = (f32[128,256]{1,0:T(8,128)S(1)}, f32[128,256]{1,0:T(8,128)S(1)}, u32[]{:S(2)}, u32[]{:S(2)}) collective-permute-start(f32[128,256]{1,0:T(8,128)S(1)} %get-tuple-element.6), channel_id=1, source_target_pairs={{0,3},{1,0},{2,1},{3,2},{4,7},{5,4},{6,5},{7,6},{8,11},{9,8},{10,9... | collective-permute-start | bytes 393224 | tf_op jit(solution)/shard_map/ppermute | solution.py:33
  52.1 4.3 %collective-permute-start.19 = (f32[256,256]{1,0:T(8,128)S(1)}, f32[256,256]{1,0:T(8,128)S(1)}, u32[]{:S(2)}, u32[]{:S(2)}) collective-permute-start(f32[256,256]{1,0:T(8,128)S(1)} %convolution_bitcast_fusion), channel_id=1, source_target_pairs={{0,8},{1,9},{2,10},{3,11},{4,12},{5,13},{6,14},{7,15},{8,0},{9,1},... | collective-permute-start | bytes 786440 | tf_op jit(solution)/shard_map/ppermute | solution.py:33
  56.4 2.7 %collective-permute-start.20 = (f32[256,256]{1,0:T(8,128)S(1)}, f32[256,256]{1,0:T(8,128)S(1)}, u32[]{:S(2)}, u32[]{:S(2)}) collective-permute-start(f32[256,256]{1,0:T(8,128)S(1)} %convolution_bitcast_fusion), channel_id=1, source_target_pairs={{0,12},{1,13},{2,14},{3,15},{4,0},{5,1},{6,2},{7,3},{8,4},{9,5},{1... | collective-permute-start | bytes 786440 | tf_op jit(solution)/shard_map/ppermute | solution.py:33
  59.5 3.0 %collective-permute-start.13 = (f32[128,256]{1,0:T(8,128)S(1)}, f32[128,256]{1,0:T(8,128)S(1)}, u32[]{:S(2)}, u32[]{:S(2)}) collective-permute-start(f32[128,256]{1,0:T(8,128)S(1)} %fusion.1), channel_id=1, source_target_pairs={{0,8},{1,9},{2,10},{3,11},{4,12},{5,13},{6,14},{7,15},{8,0},{9,1},... | collective-permute-start | bytes 393224 | tf_op jit(solution)/shard_map/ppermute | solution.py:33
  64.4 6.7 %collective-permute-done.19 = f32[256,256]{1,0:T(8,128)S(1)} collective-permute-done((f32[256,256]{1,0:T(8,128)S(1)}, f32[256,256]{1,0:T(8,128)S(1)}, u32[]{:S(2)}, u32[]{:S(2)}) %collective-permute-start.19) | collective-permute-done | bytes 262176 | tf_op jit(solution)/shard_map/ppermute | solution.py:33
  71.2 4.0 %collective-permute-done.13 = f32[128,256]{1,0:T(8,128)S(1)} collective-permute-done((f32[128,256]{1,0:T(8,128)S(1)}, f32[128,256]{1,0:T(8,128)S(1)}, u32[]{:S(2)}, u32[]{:S(2)}) %collective-permute-start.13) | collective-permute-done | bytes 131104 | tf_op jit(solution)/shard_map/ppermute | solution.py:33
  80.5 29.1 %spd_inverse.2 = f32[256,256]{1,0:T(8,128)} custom-call(f32[256,256]{1,0:T(8,128)} %mul.42.h_ref), custom_call_target="tpu_custom_call" | custom-call | flops 33554432 | bytes 524288 | tf_op jit(solution)/shard_map/spd_inverse/pallas_call | solution.py:123
  112.5 4.6 %copy-done.1 = bf16[1,1,1,3,128,128,128]{6,5,4,3,2,1,0:T(8,128)(2,1)S(1)} copy-done((bf16[1,1,1,3,128,128,128]{6,5,4,3,2,1,0:T(8,128)(2,1)S(1)}, bf16[1,1,1,3,128,128,128]{6,5,4,3,2,1,0:T(8,128)(2,1)}, u32[]{:S(2)}) %copy-start.1) | copy-done | bytes 12582936
  117.0 4.9 %mode_two.1 = f32[512,256]{1,0:T(8,128)S(1)} custom-call(s32[1]{0:T(128)} %bitcast.114.count, s32[3,3]{1,0:T(4,128)S(1)} %bitcast.122, bf16[3,128,128,128]{3,2,1,0:T(8,128)(2,1)S(1)} %bitcast.116, bf16[512,256]{1,0:T(8,128)(2,1)S(1)} %get-tuple-element.27.a_ref, bf16[512,256]{1,0:T(8,128)(2,1)S(1)} %get-tuple-element.9.c_ref), custom_call_target="tpu_custom_call" | custom-call | flops 3221225472 | bytes 12582912 | tf_op jit(solution)/shard_map/mode_two/pallas_call | solution.py:188
  122.0 11.3 %collective-permute-start.23 = (f32[128,256]{1,0:T(8,128)S(1)}, f32[128,256]{1,0:T(8,128)S(1)}, u32[]{:S(2)}, u32[]{:S(2)}) collective-permute-start(f32[128,256]{1,0:T(8,128)S(1)} %bitcast_add_fusion.1), channel_id=1, source_target_pairs={{0,64},{1,65},{2,66},{3,67},{4,68},{5,69},{6,70},{7,71},{8,72},{9,... | collective-permute-start | bytes 393224 | tf_op jit(solution)/shard_map/ppermute | solution.py:33
  133.4 14.8 %collective-permute-start.25 = (f32[128,256]{1,0:T(8,128)S(1)}, f32[128,256]{1,0:T(8,128)S(1)}, u32[]{:S(2)}, u32[]{:S(2)}) collective-permute-start(f32[128,256]{1,0:T(8,128)S(1)} %bitcast_add_fusion.1), channel_id=1, source_target_pairs={{0,192},{1,193},{2,194},{3,195},{4,196},{5,197},{6,198},{7,199},{8... | collective-permute-start | bytes 393224 | tf_op jit(solution)/shard_map/ppermute | solution.py:33
  148.7 3.1 %collective-permute-done.25 = f32[128,256]{1,0:T(8,128)S(1)} collective-permute-done((f32[128,256]{1,0:T(8,128)S(1)}, f32[128,256]{1,0:T(8,128)S(1)}, u32[]{:S(2)}, u32[]{:S(2)}) %collective-permute-start.25) | collective-permute-done | bytes 131104 | tf_op jit(solution)/shard_map/ppermute | solution.py:33
  151.8 6.3 %collective-permute-start.26 = (f32[128,256]{1,0:T(8,128)S(1)}, f32[128,256]{1,0:T(8,128)S(1)}, u32[]{:S(2)}, u32[]{:S(2)}) collective-permute-start(f32[128,256]{1,0:T(8,128)S(1)} %add_add_fusion), channel_id=1, source_target_pairs={{0,32},{1,33},{2,34},{3,35},{4,36},{5,37},{6,38},{7,39},{8,40},{9,... | collective-permute-start | bytes 393224 | tf_op jit(solution)/shard_map/ppermute | solution.py:33
  158.2 3.6 %collective-permute-start.29 = (f32[8,8,256]{2,1,0:T(8,128)S(1)}, f32[8,8,256]{2,1,0:T(8,128)S(1)}, u32[]{:S(2)}, u32[]{:S(2)}) collective-permute-start(f32[8,8,256]{2,1,0:T(8,128)S(1)} %get-tuple-element.17), channel_id=1, source_target_pairs={{0,1},{1,2},{2,3},{3,0},{4,5},{5,6},{6,7},{7,4},{8,9},{9,10},{10,1... | collective-permute-start | bytes 196616 | tf_op jit(solution)/shard_map/ppermute | solution.py:33
  164.7 2.8 %collective-permute-done.30 = f32[8,8,256]{2,1,0:T(8,128)S(1)} collective-permute-done((f32[8,8,256]{2,1,0:T(8,128)S(1)}, f32[8,8,256]{2,1,0:T(8,128)S(1)}, u32[]{:S(2)}, u32[]{:S(2)}) %collective-permute-start.30) | collective-permute-done | bytes 65568 | tf_op jit(solution)/shard_map/ppermute | solution.py:33
  167.7 8.1 %collective-permute-done.32 = f32[8,8,256]{2,1,0:T(8,128)S(1)} collective-permute-done((f32[8,8,256]{2,1,0:T(8,128)S(1)}, f32[8,8,256]{2,1,0:T(8,128)S(1)}, u32[]{:S(2)}, u32[]{:S(2)}) %collective-permute-start.32) | collective-permute-done | bytes 65568 | tf_op jit(solution)/shard_map/ppermute | solution.py:33
  176.4 3.9 %collective-permute-start.34 = (f32[8,8,256]{2,1,0:T(8,128)S(1)}, f32[8,8,256]{2,1,0:T(8,128)S(1)}, u32[]{:S(2)}, u32[]{:S(2)}) collective-permute-start(f32[8,8,256]{2,1,0:T(8,128)S(1)} %add.268), channel_id=1, source_target_pairs={{0,128},{1,129},{2,130},{3,131},{4,132},{5,133},{6,134},{7,135},{8... | collective-permute-start | bytes 196616 | tf_op jit(solution)/shard_map/ppermute | solution.py:33
  182.1 29.1 %spd_inverse.3 = f32[256,256]{1,0:T(8,128)} custom-call(f32[256,256]{1,0:T(8,128)} %select_multiply_fusion.h_ref), custom_call_target="tpu_custom_call" | custom-call | flops 33554432 | bytes 524288 | tf_op jit(solution)/shard_map/spd_inverse/pallas_call | solution.py:123
  214.3 3.3 %collective-permute-start.38 = (f32[1,256]{1,0:T(1,128)S(1)}, f32[1,256]{1,0:T(1,128)S(1)}, u32[]{:S(2)}, u32[]{:S(2)}) collective-permute-start(f32[1,256]{1,0:T(1,128)S(1)} %add.274), channel_id=1, source_target_pairs={{0,2},{1,3},{2,0},{3,1},{4,6},{5,7},{6,4},{7,5},{8,10},{9,11},{10,... | collective-permute-start | bytes 3080 | tf_op jit(solution)/shard_map/ppermute | solution.py:33
  (112 shorter events, 50.2 us)
Async XLA Ops:
  3.2 8.9 %collective-permute-start.1 = (f32[2,8,256]{2,1,0:T(8,128)S(1)}, f32[2,8,256]{2,1,0:T(8,128)S(1)}, u32[]{:S(2)}, u32[]{:S(2)}) collective-permute-start(f32[2,8,256]{2,1,0:T(8,128)S(1)} %pad_maximum_fusion.5), channel_id=1, source_target_pairs={{0,32},{1,33},{2,34},{3,35},{4,36},{5,37},{6,38},{7,39},{8,40},{9,... | collective-permute-start | bytes 49160 | tf_op jit(solution)/shard_map/ppermute | solution.py:33
  40.9 15.5 %collective-permute-start.10 = (f32[128,256]{1,0:T(8,128)S(1)}, f32[128,256]{1,0:T(8,128)S(1)}, u32[]{:S(2)}, u32[]{:S(2)}) collective-permute-start(f32[128,256]{1,0:T(8,128)S(1)} %get-tuple-element.7), channel_id=1, source_target_pairs={{0,2},{1,3},{2,0},{3,1},{4,6},{5,7},{6,4},{7,5},{8,10},{9,11},{10,... | collective-permute-start | bytes 393224 | tf_op jit(solution)/shard_map/ppermute | solution.py:33
  42.5 16.7 %collective-permute-start.11 = (f32[128,256]{1,0:T(8,128)S(1)}, f32[128,256]{1,0:T(8,128)S(1)}, u32[]{:S(2)}, u32[]{:S(2)}) collective-permute-start(f32[128,256]{1,0:T(8,128)S(1)} %get-tuple-element.6), channel_id=1, source_target_pairs={{0,3},{1,0},{2,1},{3,2},{4,7},{5,4},{6,5},{7,6},{8,11},{9,8},{10,9... | collective-permute-start | bytes 393224 | tf_op jit(solution)/shard_map/ppermute | solution.py:33
  52.0 10.5 %collective-permute-start.18 = (f32[256,256]{1,0:T(8,128)S(1)}, f32[256,256]{1,0:T(8,128)S(1)}, u32[]{:S(2)}, u32[]{:S(2)}) collective-permute-start(f32[256,256]{1,0:T(8,128)S(1)} %convolution_bitcast_fusion), channel_id=1, source_target_pairs={{0,4},{1,5},{2,6},{3,7},{4,8},{5,9},{6,10},{7,11},{8,12},{9,13},{1... | collective-permute-start | bytes 786440 | tf_op jit(solution)/shard_map/ppermute | solution.py:33
  52.1 18.9 %collective-permute-start.19 = (f32[256,256]{1,0:T(8,128)S(1)}, f32[256,256]{1,0:T(8,128)S(1)}, u32[]{:S(2)}, u32[]{:S(2)}) collective-permute-start(f32[256,256]{1,0:T(8,128)S(1)} %convolution_bitcast_fusion), channel_id=1, source_target_pairs={{0,8},{1,9},{2,10},{3,11},{4,12},{5,13},{6,14},{7,15},{8,0},{9,1},... | collective-permute-start | bytes 786440 | tf_op jit(solution)/shard_map/ppermute | solution.py:33
  56.4 14.6 %collective-permute-start.20 = (f32[256,256]{1,0:T(8,128)S(1)}, f32[256,256]{1,0:T(8,128)S(1)}, u32[]{:S(2)}, u32[]{:S(2)}) collective-permute-start(f32[256,256]{1,0:T(8,128)S(1)} %convolution_bitcast_fusion), channel_id=1, source_target_pairs={{0,12},{1,13},{2,14},{3,15},{4,0},{5,1},{6,2},{7,3},{8,4},{9,5},{1... | collective-permute-start | bytes 786440 | tf_op jit(solution)/shard_map/ppermute | solution.py:33
  59.2 12.0 %collective-permute-start.12 = (f32[128,256]{1,0:T(8,128)S(1)}, f32[128,256]{1,0:T(8,128)S(1)}, u32[]{:S(2)}, u32[]{:S(2)}) collective-permute-start(f32[128,256]{1,0:T(8,128)S(1)} %fusion.1), channel_id=1, source_target_pairs={{0,4},{1,5},{2,6},{3,7},{4,8},{5,9},{6,10},{7,11},{8,12},{9,13},{1... | collective-permute-start | bytes 393224 | tf_op jit(solution)/shard_map/ppermute | solution.py:33
  59.5 15.7 %collective-permute-start.13 = (f32[128,256]{1,0:T(8,128)S(1)}, f32[128,256]{1,0:T(8,128)S(1)}, u32[]{:S(2)}, u32[]{:S(2)}) collective-permute-start(f32[128,256]{1,0:T(8,128)S(1)} %fusion.1), channel_id=1, source_target_pairs={{0,8},{1,9},{2,10},{3,11},{4,12},{5,13},{6,14},{7,15},{8,0},{9,1},... | collective-permute-start | bytes 393224 | tf_op jit(solution)/shard_map/ppermute | solution.py:33
  62.5 12.8 %collective-permute-start.14 = (f32[128,256]{1,0:T(8,128)S(1)}, f32[128,256]{1,0:T(8,128)S(1)}, u32[]{:S(2)}, u32[]{:S(2)}) collective-permute-start(f32[128,256]{1,0:T(8,128)S(1)} %fusion.1), channel_id=1, source_target_pairs={{0,12},{1,13},{2,14},{3,15},{4,0},{5,1},{6,2},{7,3},{8,4},{9,5},{1... | collective-permute-start | bytes 393224 | tf_op jit(solution)/shard_map/ppermute | solution.py:33
  71.1 8.7 %collective-permute-start.21 = (f32[256,256]{1,0:T(8,128)S(1)}, f32[256,256]{1,0:T(8,128)S(1)}, u32[]{:S(2)}, u32[]{:S(2)}) collective-permute-start(f32[256,256]{1,0:T(8,128)S(1)} %add_multiply_fusion), channel_id=1, source_target_pairs={{0,16},{1,17},{2,18},{3,19},{4,20},{5,21},{6,22},{7,23},{8,24},{9,... | collective-permute-start | bytes 786440 | tf_op jit(solution)/shard_map/ppermute | solution.py:33
  75.3 34.4 %collective-permute-start.15 = (f32[128,256]{1,0:T(8,128)S(1)}, f32[128,256]{1,0:T(8,128)S(1)}, u32[]{:S(2)}, u32[]{:S(2)}) collective-permute-start(f32[128,256]{1,0:T(8,128)S(1)} %add_add_fusion.1), channel_id=1, source_target_pairs={{0,1},{1,2},{2,3},{3,0},{4,5},{5,6},{6,7},{7,4},{8,9},{9,10},{10,1... | collective-permute-start | bytes 393224 | tf_op jit(solution)/shard_map/ppermute | solution.py:33
  76.6 33.1 %collective-permute-start.16 = (f32[128,256]{1,0:T(8,128)S(1)}, f32[128,256]{1,0:T(8,128)S(1)}, u32[]{:S(2)}, u32[]{:S(2)}) collective-permute-start(f32[128,256]{1,0:T(8,128)S(1)} %add_add_fusion.1), channel_id=1, source_target_pairs={{0,2},{1,3},{2,0},{3,1},{4,6},{5,7},{6,4},{7,5},{8,10},{9,11},{10,... | collective-permute-start | bytes 393224 | tf_op jit(solution)/shard_map/ppermute | solution.py:33
  78.8 30.8 %collective-permute-start.17 = (f32[128,256]{1,0:T(8,128)S(1)}, f32[128,256]{1,0:T(8,128)S(1)}, u32[]{:S(2)}, u32[]{:S(2)}) collective-permute-start(f32[128,256]{1,0:T(8,128)S(1)} %add_add_fusion.1), channel_id=1, source_target_pairs={{0,3},{1,0},{2,1},{3,2},{4,7},{5,4},{6,5},{7,6},{8,11},{9,8},{10,9... | collective-permute-start | bytes 393224 | tf_op jit(solution)/shard_map/ppermute | solution.py:33
  112.4 9.6 %collective-permute-start.22 = (f32[128,256]{1,0:T(8,128)S(1)}, f32[128,256]{1,0:T(8,128)S(1)}, u32[]{:S(2)}, u32[]{:S(2)}) collective-permute-start(f32[128,256]{1,0:T(8,128)S(1)} %dynamic-slice_bitcast_fusion.1), channel_id=1, source_target_pairs={{0,16},{1,17},{2,18},{3,19},{4,20},{5,21},{6,22},{7,23},{8,24},{9,... | collective-permute-start | bytes 393224 | tf_op jit(solution)/shard_map/ppermute | solution.py:33
  122.0 26.7 %collective-permute-start.23 = (f32[128,256]{1,0:T(8,128)S(1)}, f32[128,256]{1,0:T(8,128)S(1)}, u32[]{:S(2)}, u32[]{:S(2)}) collective-permute-start(f32[128,256]{1,0:T(8,128)S(1)} %bitcast_add_fusion.1), channel_id=1, source_target_pairs={{0,64},{1,65},{2,66},{3,67},{4,68},{5,69},{6,70},{7,71},{8,72},{9,... | collective-permute-start | bytes 393224 | tf_op jit(solution)/shard_map/ppermute | solution.py:33
  133.4 15.3 %collective-permute-start.24 = (f32[128,256]{1,0:T(8,128)S(1)}, f32[128,256]{1,0:T(8,128)S(1)}, u32[]{:S(2)}, u32[]{:S(2)}) collective-permute-start(f32[128,256]{1,0:T(8,128)S(1)} %bitcast_add_fusion.1), channel_id=1, source_target_pairs={{0,128},{1,129},{2,130},{3,131},{4,132},{5,133},{6,134},{7,135},{8... | collective-permute-start | bytes 393224 | tf_op jit(solution)/shard_map/ppermute | solution.py:33
  133.4 18.4 %collective-permute-start.25 = (f32[128,256]{1,0:T(8,128)S(1)}, f32[128,256]{1,0:T(8,128)S(1)}, u32[]{:S(2)}, u32[]{:S(2)}) collective-permute-start(f32[128,256]{1,0:T(8,128)S(1)} %bitcast_add_fusion.1), channel_id=1, source_target_pairs={{0,192},{1,193},{2,194},{3,195},{4,196},{5,197},{6,198},{7,199},{8... | collective-permute-start | bytes 393224 | tf_op jit(solution)/shard_map/ppermute | solution.py:33
  148.2 9.9 %collective-permute-start.28 = (f32[4,8,8,256]{3,2,0,1:T(8,128)S(1)}, f32[4,8,8,256]{3,2,0,1:T(8,128)S(1)}, u32[]{:S(2)}, u32[]{:S(2)}) collective-permute-start(f32[4,8,8,256]{3,2,0,1:T(8,128)S(1)} %dynamic-slice_bitcast_fusion), channel_id=1, source_target_pairs={{0,16},{1,17},{2,18},{3,19},{4,20},{5,21},{6,22},{7,23},{8,24},{9,... | collective-permute-start | bytes 786440 | tf_op jit(solution)/shard_map/ppermute | solution.py:33
  151.8 12.8 %collective-permute-start.26 = (f32[128,256]{1,0:T(8,128)S(1)}, f32[128,256]{1,0:T(8,128)S(1)}, u32[]{:S(2)}, u32[]{:S(2)}) collective-permute-start(f32[128,256]{1,0:T(8,128)S(1)} %add_add_fusion), channel_id=1, source_target_pairs={{0,32},{1,33},{2,34},{3,35},{4,36},{5,37},{6,38},{7,39},{8,40},{9,... | collective-permute-start | bytes 393224 | tf_op jit(solution)/shard_map/ppermute | solution.py:33
  164.6 16.5 %collective-permute-start.27 = (f32[128,256]{1,0:T(8,128)S(1)}, f32[128,256]{1,0:T(8,128)S(1)}, u32[]{:S(2)}, u32[]{:S(2)}) collective-permute-start(f32[128,256]{1,0:T(8,128)S(1)} %add.261), channel_id=1, source_target_pairs={{0,16},{1,17},{2,18},{3,19},{4,20},{5,21},{6,22},{7,23},{8,24},{9,... | collective-permute-start | bytes 393224 | tf_op jit(solution)/shard_map/ppermute | solution.py:33
  167.6 8.3 %collective-permute-start.32 = (f32[8,8,256]{2,1,0:T(8,128)S(1)}, f32[8,8,256]{2,1,0:T(8,128)S(1)}, u32[]{:S(2)}, u32[]{:S(2)}) collective-permute-start(f32[8,8,256]{2,1,0:T(8,128)S(1)} %fusion.3), channel_id=1, source_target_pairs={{0,32},{1,33},{2,34},{3,35},{4,36},{5,37},{6,38},{7,39},{8,40},{9,... | collective-permute-start | bytes 196616 | tf_op jit(solution)/shard_map/ppermute | solution.py:33
  175.9 35.3 %collective-permute-start.33 = (f32[8,8,256]{2,1,0:T(8,128)S(1)}, f32[8,8,256]{2,1,0:T(8,128)S(1)}, u32[]{:S(2)}, u32[]{:S(2)}) collective-permute-start(f32[8,8,256]{2,1,0:T(8,128)S(1)} %add.268), channel_id=1, source_target_pairs={{0,64},{1,65},{2,66},{3,67},{4,68},{5,69},{6,70},{7,71},{8,72},{9,... | collective-permute-start | bytes 196616 | tf_op jit(solution)/shard_map/ppermute | solution.py:33
  176.4 34.8 %collective-permute-start.34 = (f32[8,8,256]{2,1,0:T(8,128)S(1)}, f32[8,8,256]{2,1,0:T(8,128)S(1)}, u32[]{:S(2)}, u32[]{:S(2)}) collective-permute-start(f32[8,8,256]{2,1,0:T(8,128)S(1)} %add.268), channel_id=1, source_target_pairs={{0,128},{1,129},{2,130},{3,131},{4,132},{5,133},{6,134},{7,135},{8... | collective-permute-start | bytes 196616 | tf_op jit(solution)/shard_map/ppermute | solution.py:33
  180.3 30.9 %collective-permute-start.35 = (f32[8,8,256]{2,1,0:T(8,128)S(1)}, f32[8,8,256]{2,1,0:T(8,128)S(1)}, u32[]{:S(2)}, u32[]{:S(2)}) collective-permute-start(f32[8,8,256]{2,1,0:T(8,128)S(1)} %add.268), channel_id=1, source_target_pairs={{0,192},{1,193},{2,194},{3,195},{4,196},{5,197},{6,198},{7,199},{8... | collective-permute-start | bytes 196616 | tf_op jit(solution)/shard_map/ppermute | solution.py:33
  (21 other events, 99.6 us)
